TPU v7x, 32 devices: a whole 2x2x4 slice. The times are simulated.
32 devices in a mesh: groups: 2 (over y), space: 4 (over z), tangent: 4 (over x, core).
Axes of the slice: x: 2, y: 2, z: 4, core: 2. Of those that a mesh axis runs over, the one named last changes fastest.
Arguments:
- positions: float32 [16, 2, 128], P(('groups', 'space')), parts along dimension 0, may hold values from 0.45 to 15.55, as said below
- momenta: float32 [16, 2, 128], P(('groups', 'space')), parts along dimension 0, may hold values from -4 to 4
- cell_count: int32 [16], P(('groups', 'space')), parts along dimension 0, may hold values from 64 to 128, as said below
- tangent: float32 [16, 4, 128, 1024], P(('groups', 'space'), None, None, 'tangent'), parts along dimension 0, may hold values from -6 to 6
Outputs:
- phase: float32 [16, 4, 128], P(('groups', 'space')), parts along dimension 0
- new_tangent: float32 [16, 4, 128, 1024], P(('groups', 'space'), None, None, 'tangent'), parts along dimension 0
- stretch: float32 [2048], P(('groups', 'tangent')), parts along dimension 0
There are 2 independent parts, one for each index of `groups`. A program takes and returns all parts, laid end to end along the dimension named above; each array names one. Nothing has to cross between parts.
Inputs may be any that keep to these rules, and one draw needn't show every extreme that they name: Slots 0 to cell_count - 1 of a cell hold particles, the others are padding; some cell holds 128 particles in every draw. `positions`: every slot of a cell, padding too, lies within 0.05 in each coordinate of its own point of the lattice (m + 0.5, n + 0.5), m from 0 to 7, n from 0 to 15; no two slots of a cell share a lattice point.
All inputs are finite; a program needn't handle non-finite values.
Results may differ from a plain program's by a relative error of at most 0.006.
Values may be sent and summed in bfloat16 or wider, within the bound.
No kernel may reach another device: no remote copies, remote signals or barrier semaphores. Data moves between devices by JAX's collectives and lax.ppermute only.
A program may use at most 128 MiB of HBM per device.

v0:
```python
import jax
import jax.numpy as jnp
from jax import lax
from jax.sharding import PartitionSpec as P

STEPS = 2
DT = 0.005
CUT2 = 2.0 ** (1.0 / 3.0)
PARK = 1000.0
HIGH = lax.Precision.HIGHEST


def padded(block, sides, width):
    for axis, dim in sides:
        count = lax.axis_size(axis)
        forward = [(i, i + 1) for i in range(count - 1)]
        forward.append((count - 1, 0))
        backward = [(target, source) for source, target in forward]
        low = lax.ppermute(
            lax.slice_in_dim(block, block.shape[dim] - width, None, axis=dim), axis, forward
        )
        high = lax.ppermute(lax.slice_in_dim(block, 0, width, axis=dim), axis, backward)
        block = jnp.concatenate([low, block, high], axis=dim)
    return block


def pair_terms(own_coords, own_alive, far_coords, shift_x, shift_y, same_cell):
    delta_x = shift_x + far_coords[:, 0, None, :] - own_coords[:, 0, :, None]
    delta_y = shift_y + far_coords[:, 1, None, :] - own_coords[:, 1, :, None]
    dist2 = delta_x * delta_x + delta_y * delta_y
    within = jnp.logical_and(dist2 < CUT2, own_alive[:, :, None] > 0.5)
    if same_cell:
        within = jnp.logical_and(within, jnp.logical_not(jnp.eye(dist2.shape[-1], dtype=bool)))
    weight = within.astype(jnp.float32)
    safe = jnp.where(within, dist2, CUT2)
    inverse = 1.0 / safe
    inv_three = inverse * inverse * inverse
    inv_six = inv_three * inv_three
    energy = 4.0 * (inv_six - inv_three) + 1.0
    energy_1 = 4.0 * (3.0 * inv_three - 6.0 * inv_six) * inverse
    energy_2 = 4.0 * (42.0 * inv_six - 12.0 * inv_three) * inverse * inverse
    taper = 1.0 - safe / CUT2
    switch = taper * taper
    switch_1 = -2.0 * taper / CUT2
    switch_2 = 2.0 / (CUT2 * CUT2)
    grad_1 = (energy_1 * switch + energy * switch_1) * weight
    grad_2 = (energy_2 * switch + 2.0 * energy_1 * switch_1 + energy * switch_2) * weight
    pull_x = 2.0 * grad_1 * delta_x
    pull_y = 2.0 * grad_1 * delta_y
    k_xx = (2.0 * grad_1 + 4.0 * grad_2 * delta_x * delta_x).astype(jnp.bfloat16)
    k_xy = (4.0 * grad_2 * delta_x * delta_y).astype(jnp.bfloat16)
    k_yy = (2.0 * grad_1 + 4.0 * grad_2 * delta_y * delta_y).astype(jnp.bfloat16)
    return (pull_x, pull_y, k_xx, k_xy, k_yy)


def apply_rows(k_xx, k_xy, k_yy, far_low):
    gain_x = jnp.einsum(
        "cij,cjv->civ", k_xx, far_low[:, 0], preferred_element_type=jnp.float32
    ) + jnp.einsum("cij,cjv->civ", k_xy, far_low[:, 1], preferred_element_type=jnp.float32)
    gain_y = jnp.einsum(
        "cij,cjv->civ", k_xy, far_low[:, 0], preferred_element_type=jnp.float32
    ) + jnp.einsum("cij,cjv->civ", k_yy, far_low[:, 1], preferred_element_type=jnp.float32)
    return (gain_x, gain_y)


def add_pair(totals, parked, occupied, far_coords, far_low, shift_x, shift_y, same_cell):
    forces_x, forces_y, push_x, push_y, diag_xx, diag_xy, diag_yy = totals
    pull_x, pull_y, k_xx, k_xy, k_yy = pair_terms(
        parked, occupied, far_coords, shift_x, shift_y, same_cell
    )
    gain_x, gain_y = apply_rows(k_xx, k_xy, k_yy, far_low)
    totals = (
        forces_x + jnp.sum(pull_x, axis=2),
        forces_y + jnp.sum(pull_y, axis=2),
        push_x + gain_x,
        push_y + gain_y,
        diag_xx + jnp.sum(k_xx.astype(jnp.float32), axis=2),
        diag_xy + jnp.sum(k_xy.astype(jnp.float32), axis=2),
        diag_yy + jnp.sum(k_yy.astype(jnp.float32), axis=2),
    )
    return (totals, (pull_x, pull_y, k_xx, k_xy, k_yy))


def evaluate(coords, occupied, small_q):
    cell_total = coords.shape[0]
    low = small_q.astype(jnp.bfloat16)
    parked = jnp.concatenate(
        [coords[:, 0:1] + PARK * (1.0 - occupied)[:, None, :], coords[:, 1:2]], axis=1
    )
    empty_rows = jnp.zeros(occupied.shape, jnp.float32)
    empty_push = jnp.zeros(small_q[:, 0].shape, jnp.float32)
    totals = (empty_rows, empty_rows, empty_push, empty_push, empty_rows, empty_rows, empty_rows)
    far_low = padded(low, (("space", 0),), cell_total)
    far_coords = padded(parked, (("space", 0),), cell_total)
    for side in (-1, 0, 1):
        if side == 0:
            block_low = low
            block_coords = parked
        else:
            begin = (1 + side) * cell_total
            block_low = far_low[begin : begin + cell_total]
            block_coords = far_coords[begin : begin + cell_total]
        for lane in (-1, 0, 1):
            totals, unused = add_pair(
                totals,
                parked,
                occupied,
                jnp.roll(block_coords, -lane, axis=0),
                jnp.roll(block_low, -lane, axis=0),
                8.0 * side,
                16.0 * lane,
                side == 0 and lane == 0,
            )
    forces_x, forces_y, push_x, push_y, diag_xx, diag_xy, diag_yy = totals
    wide_own = low.astype(jnp.float32)
    push_x = push_x - diag_xx[..., None] * wide_own[:, 0] - diag_xy[..., None] * wide_own[:, 1]
    push_y = push_y - diag_xy[..., None] * wide_own[:, 0] - diag_yy[..., None] * wide_own[:, 1]
    forces = jnp.stack([forces_x, forces_y], axis=1)
    pushes = jnp.stack([push_x, push_y], axis=1)
    return (forces, pushes)


def body(positions, momenta, cell_count, tangent):
    cell_total = positions.shape[0]
    slot_count = positions.shape[2]
    block_cols = tangent.shape[3]
    occupied = (
        lax.broadcasted_iota(jnp.int32, (cell_total, slot_count), 1) < cell_count[:, None]
    ).astype(jnp.float32)
    state = tangent * occupied[:, None, :, None]
    coords = positions
    speeds = momenta
    small_q = state[:, 0:2]
    small_p = state[:, 2:4]
    forces, pushes = evaluate(coords, occupied, small_q)
    for step_index in range(STEPS):
        midway_p = speeds + 0.5 * DT * forces
        midway_dp = small_p + 0.5 * DT * pushes
        coords = coords + DT * midway_p
        small_q = small_q + DT * midway_dp
        forces, pushes = evaluate(coords, occupied, small_q)
        speeds = midway_p + 0.5 * DT * forces
        small_p = midway_dp + 0.5 * DT * pushes
    phase = jnp.concatenate([coords, speeds], axis=1)
    final = jnp.concatenate([small_q, small_p], axis=1)
    rows_form = lax.all_to_all(final, "tangent", split_axis=2, concat_axis=3, tiled=True)
    full_width = rows_form.shape[3]
    flat_rows = rows_form.reshape(-1, full_width)
    partial_value = lax.dot_general(
        flat_rows,
        flat_rows,
        (((0,), (0,)), ((), ())),
        precision=HIGH,
        preferred_element_type=jnp.float32,
    )
    gram_scale = 1.0 / (4.0 * slot_count * cell_total * lax.axis_size("space"))
    gram = lax.psum(partial_value, ("space", "tangent"))
    factor = jnp.linalg.cholesky(gram * gram_scale)
    solved = jax.scipy.linalg.solve_triangular(factor, flat_rows.T, lower=True).T
    columns_out = lax.all_to_all(
        solved.reshape(rows_form.shape), "tangent", split_axis=3, concat_axis=2, tiled=True
    )
    log_diag = jnp.log(jnp.diagonal(factor))
    stretch = lax.dynamic_slice_in_dim(log_diag, lax.axis_index("tangent") * block_cols, block_cols)
    return (phase, columns_out, stretch)


def solution(mesh):
    placed = (
        P(("groups", "space"), None, None),
        P(("groups", "space"), None, None),
        P(("groups", "space")),
        P(("groups", "space"), None, None, "tangent"),
    )
    return jax.shard_map(
        body,
        mesh=mesh,
        in_specs=placed,
        out_specs=(
            P(("groups", "space"), None, None),
            P(("groups", "space"), None, None, "tangent"),
            P(("groups", "tangent")),
        ),
        check_vma=False,
    )
```

profile of v0, /device:TPU:1, one launch (start us, length us, event | category | flops | bytes accessed | tf_op | source)
XLA Modules:
  0.0 639.7 jit_solution(17771305510368086692)
XLA Ops:
  8.1 4.2 collective-permute-start.1
  14.4 3.3 collective-permute-start.7
  20.4 3.1 convert_reduce_fusion.79
  23.7 3.3 collective-permute-start.3
  27.9 3.4 collective-permute-done.2
  31.3 3.1 convert_reduce_fusion.52
  37.1 2.1 collective-permute-done.4
  39.3 3.3 convert_reduce_fusion.25
  58.0 1.5 collective-permute-start.8
  59.8 4.8 collective-permute-done.9
  82.1 2.7 collective-permute-done.11
  86.5 7.0 %collective-permute-done.10 = bf16[2,2,128,256]{3,2,0,1:T(8,128)(2,1)S(1)} collective-permute-done((bf16[2,2,128,256]{3,2,0,1:T(8,128)(2,1)S(1)}, bf16[2,2,128,256]{3,2,0,1:T(8,128)(2,1)S(1)}, u32[]{:S(2)}, u32[]{:S(2)}) %collective-permute-start.10) | collective-permute-done | bytes 262176 | tf_op jit(solution)/shard_map/ppermute | solution.py:19
  105.5 21.8 %all_to_all.33 = f32[2,4,128,256]{3,0,1,2:T(2,128)S(1)} all-to-all(f32[2,4,128,256]{3,0,1,2:T(2,128)S(1)} %copy.18), channel_id=1, replica_groups=mesh['groups'=2,'space'=4,'tangent'=4] {'tangent'}, dimensions={2} | all-to-all | bytes 2097152 | tf_op jit(solution)/shard_map/all_to_all | solution.py:146
  128.2 5.2 fusion.2420
  133.8 107.8 %all-reduce.3.cloned.1.call-done = f32[1024,1024]{0,1:T(8,128)} async-done(((f32[1024,1024]{0,1:T(8,128)}), f32[1024,1024]{0,1:T(8,128)}) %all-reduce.3.cloned.1.call-update) | async-done | bytes 4194320 | tf_op jit(solution)/shard_map/psum | solution.py:157
  241.6 5.0 broadcast_multiply_fusion
  246.6 5.7 copy.21
  252.3 4.4 fusion
  256.8 1.9 copy-done
  258.7 11.7 %cholesky.187 = f32[128,128]{1,0:T(8,128)S(1)} custom-call(f32[128,128]{1,0:T(8,128)S(1)} %cholesky.514), custom_call_target="Cholesky" | custom-call | tf_op jit(solution)/shard_map/jit(cholesky)/cholesky | solution.py:158
  271.1 9.8 %custom-call.63 = f32[1,128,128]{1,2,0:T(8,128)S(1)} custom-call(f32[1,128,128]{2,1,0:T(8,128)S(1)} %get-tuple-element.432), custom_call_target="InvertDiagBlocksLowerTriangular" | custom-call | tf_op jit(solution)/shard_map/jit(cholesky)/cholesky | solution.py:158
  280.9 2.5 cholesky.218
  283.4 2.3 constant_dynamic-update-slice_fusion.32
  285.7 1.5 convolution_subtract_fusion
  287.3 11.9 %cholesky.209 = f32[128,128]{1,0:T(8,128)S(1)} custom-call(f32[128,128]{1,0:T(8,128)S(1)} %cholesky.518), custom_call_target="Cholesky" | custom-call | tf_op jit(solution)/shard_map/jit(cholesky)/cholesky | solution.py:158
  300.5 9.8 %custom-call.64 = f32[1,128,128]{1,2,0:T(8,128)S(1)} custom-call(f32[1,128,128]{2,1,0:T(8,128)S(1)} %get-tuple-element.429), custom_call_target="InvertDiagBlocksLowerTriangular" | custom-call | tf_op jit(solution)/shard_map/jit(cholesky)/cholesky | solution.py:158
  311.5 2.1 convolution_subtract_fusion.1
  313.6 11.7 %cholesky.402 = f32[128,128]{1,0:T(8,128)S(1)} custom-call(f32[128,128]{1,0:T(8,128)S(1)} %cholesky.523), custom_call_target="Cholesky" | custom-call | tf_op jit(solution)/shard_map/jit(cholesky)/cholesky | solution.py:158
  326.6 9.8 %custom-call.65 = f32[1,128,128]{1,2,0:T(8,128)S(1)} custom-call(f32[1,128,128]{2,1,0:T(8,128)S(1)} %get-tuple-element.426), custom_call_target="InvertDiagBlocksLowerTriangular" | custom-call | tf_op jit(solution)/shard_map/jit(cholesky)/cholesky | solution.py:158
  337.6 2.4 convolution_subtract_fusion.2
  340.0 11.9 %cholesky.421 = f32[128,128]{1,0:T(8,128)S(1)} custom-call(f32[128,128]{1,0:T(8,128)S(1)} %cholesky.528), custom_call_target="Cholesky" | custom-call | tf_op jit(solution)/shard_map/jit(cholesky)/cholesky | solution.py:158
  353.3 9.8 %custom-call.66 = f32[1,128,128]{1,2,0:T(8,128)S(1)} custom-call(f32[1,128,128]{2,1,0:T(8,128)S(1)} %get-tuple-element.423), custom_call_target="InvertDiagBlocksLowerTriangular" | custom-call | tf_op jit(solution)/shard_map/jit(cholesky)/cholesky | solution.py:158
  364.2 2.3 convolution_subtract_fusion.3
  366.5 11.7 %cholesky.440 = f32[128,128]{1,0:T(8,128)S(1)} custom-call(f32[128,128]{1,0:T(8,128)S(1)} %cholesky.533), custom_call_target="Cholesky" | custom-call | tf_op jit(solution)/shard_map/jit(cholesky)/cholesky | solution.py:158
  379.6 10.2 %custom-call.67 = f32[1,128,128]{1,2,0:T(8,128)S(1)} custom-call(f32[1,128,128]{2,1,0:T(8,128)S(1)} %get-tuple-element.420), custom_call_target="InvertDiagBlocksLowerTriangular" | custom-call | tf_op jit(solution)/shard_map/jit(cholesky)/cholesky | solution.py:158
  390.8 2.3 convolution_subtract_fusion.4
  393.1 11.7 %cholesky.460 = f32[128,128]{1,0:T(8,128)S(1)} custom-call(f32[128,128]{1,0:T(8,128)S(1)} %cholesky.538), custom_call_target="Cholesky" | custom-call | tf_op jit(solution)/shard_map/jit(cholesky)/cholesky | solution.py:158
  406.1 9.8 %custom-call.68 = f32[1,128,128]{1,2,0:T(8,128)S(1)} custom-call(f32[1,128,128]{2,1,0:T(8,128)S(1)} %get-tuple-element.417), custom_call_target="InvertDiagBlocksLowerTriangular" | custom-call | tf_op jit(solution)/shard_map/jit(cholesky)/cholesky | solution.py:158
  416.9 2.0 convolution_subtract_fusion.11
  418.9 11.9 %cholesky.480 = f32[128,128]{1,0:T(8,128)S(1)} custom-call(f32[128,128]{1,0:T(8,128)S(1)} %cholesky.543), custom_call_target="Cholesky" | custom-call | tf_op jit(solution)/shard_map/jit(cholesky)/cholesky | solution.py:158
  432.1 9.8 %custom-call.69 = f32[1,128,128]{1,2,0:T(8,128)S(1)} custom-call(f32[1,128,128]{2,1,0:T(8,128)S(1)} %get-tuple-element.414), custom_call_target="InvertDiagBlocksLowerTriangular" | custom-call | tf_op jit(solution)/shard_map/jit(cholesky)/cholesky | solution.py:158
  442.7 1.8 convolution_subtract_fusion.13
  444.5 11.7 %cholesky.498 = f32[128,128]{1,0:T(8,128)S(1)} custom-call(f32[128,128]{1,0:T(8,128)S(1)} %convolution_subtract_fusion.13), custom_call_target="Cholesky" | custom-call | tf_op jit(solution)/shard_map/jit(cholesky)/cholesky | solution.py:158
  462.6 6.6 %fusion.1 = (f32[1024,1024]{1,0:T(8,128)}, f32[1024,1024]{1,0:T(8,128)}) fusion(f32[1024,1024]{1,0:T(8,128)} %get-tuple-element.412, pred[]{:T(512)S(6)} %cholesky.513), kind=kLoop, calls=%fused_computation.7 | loop fusion | flops 4194304 | bytes 12582913 | tf_op jit(solution)/shard_map/jit(_solve_triangular)/triangular_solve | solution.py:159
  469.2 23.2 %while.1 = (s32[]{:T(128)}, f32[1024,1024]{1,0:T(8,128)}, s32[8,2]{0,1:T(2,128)S(1)}, f32[8,128,128]{2,1,0:T(8,128)S(1)}, s32[]{:T(128)}) while((s32[]{:T(128)}, f32[1024,1024]{1,0:T(8,128)}, s32[8,2]{0,1:T(2,128)S(1)}, f32[8,128,128]{2,1,0:T(8,128)S(1)}, s32[]{:T(128)}) %tuple.396), condition=%wide.while_cond, body=%wide.while_body.sunk | while | flops 2 | bytes 131189 | solution.py:159
  469.8 2.3 bitcast_dynamic-update-slice_fusion.2
  472.7 2.3 bitcast_dynamic-update-slice_fusion.2
  475.6 2.3 bitcast_dynamic-update-slice_fusion.2
  478.5 2.3 bitcast_dynamic-update-slice_fusion.2
  481.4 2.3 bitcast_dynamic-update-slice_fusion.2
  484.4 2.3 bitcast_dynamic-update-slice_fusion.2
  487.3 2.3 bitcast_dynamic-update-slice_fusion.2
  490.2 2.2 bitcast_dynamic-update-slice_fusion.2
  492.4 79.4 %custom-call.70 = f32[8,128,128]{1,2,0:T(8,128)} custom-call(f32[8,128,128]{2,1,0:T(8,128)S(1)} %get-tuple-element.10), custom_call_target="InvertDiagBlocksLowerTriangular" | custom-call | tf_op jit(solution)/shard_map/jit(_solve_triangular)/triangular_solve | solution.py:159
  581.1 1.5 convolution_subtract_fusion.5
  582.9 1.5 convolution_subtract_fusion.9
  584.7 1.6 convolution_subtract_fusion.12
  587.0 3.1 copy.24
  590.1 5.3 reshape.847
  595.5 5.5 all-to-all-start.1
  601.7 17.3 %gather_fusion = f32[1024]{0:T(1024)S(1)} fusion(f32[1024,1024]{1,0:T(8,128)} %get-tuple-element.320, s32[1024]{0:T(1024)S(1)} %bitcast.397), kind=kCustom, calls=%fused_computation | custom fusion | bytes 16384 | tf_op jit(solution)/shard_map/jit(diagonal)/cond/branch_0_fun/gather | solution.py:163
  620.2 3.7 reduce.48
  623.8 4.2 reshape.848
  628.1 4.6 copy.25
  (286 shorter events, 90.3 us)
Async XLA Ops:
  7.2 234.4 %all-reduce.3.cloned.1.call-start = ((), (), s32[]{:S(2)}) async-start(), calls=%async_computation.2 | async-start | bytes 8388608 | tf_op jit(solution)/shard_map/psum | solution.py:157
  8.1 12.2 %collective-permute-start.1 = (f32[2,2,128]{2,1,0:T(2,128)S(1)}, f32[2,2,128]{2,1,0:T(2,128)S(1)}, u32[]{:S(2)}, u32[]{:S(2)}) collective-permute-start(f32[2,2,128]{2,1,0:T(2,128)S(1)} %pad_maximum_fusion.11), channel_id=1, source_target_pairs={{4,0},{8,4},{12,8},{0,12},{5,1},{9,5},{13,9},{1,13},{6,2},{10,6},{... | collective-permute-start | bytes 6152 | tf_op jit(solution)/shard_map/ppermute | solution.py:22
  12.3 8.1 %collective-permute-start = (f32[2,2,128]{2,1,0:T(2,128)S(1)}, f32[2,2,128]{2,1,0:T(2,128)S(1)}, u32[]{:S(2)}, u32[]{:S(2)}) collective-permute-start(f32[2,2,128]{2,1,0:T(2,128)S(1)} %pad_maximum_fusion.11), channel_id=1, source_target_pairs={{0,4},{4,8},{8,12},{12,0},{1,5},{5,9},{9,13},{13,1},{2,6},{6,10},{... | collective-permute-start | bytes 6152 | tf_op jit(solution)/shard_map/ppermute | solution.py:19
  14.4 28.2 %collective-permute-start.7 = (bf16[2,2,128,256]{3,2,0,1:T(8,128)(2,1)S(1)}, bf16[2,2,128,256]{3,2,0,1:T(8,128)(2,1)S(1)}, u32[]{:S(2)}, u32[]{:S(2)}) collective-permute-start(bf16[2,2,128,256]{3,2,0,1:T(8,128)(2,1)S(1)} %get-tuple-element.327), channel_id=1, source_target_pairs={{4,0},{8,4},{12,8},{0,12},{5,1},{9,5},{13,9},{1,13},{6,2},{10,6},{... | collective-permute-start | bytes 786440 | tf_op jit(solution)/shard_map/ppermute | solution.py:22
  17.7 26.6 %collective-permute-start.6 = (bf16[2,2,128,256]{3,2,0,1:T(8,128)(2,1)S(1)}, bf16[2,2,128,256]{3,2,0,1:T(8,128)(2,1)S(1)}, u32[]{:S(2)}, u32[]{:S(2)}) collective-permute-start(bf16[2,2,128,256]{3,2,0,1:T(8,128)(2,1)S(1)} %get-tuple-element.327), channel_id=1, source_target_pairs={{0,4},{4,8},{8,12},{12,0},{1,5},{5,9},{9,13},{13,1},{2,6},{6,10},{... | collective-permute-start | bytes 786440 | tf_op jit(solution)/shard_map/ppermute | solution.py:19
  18.6 4.9 copy-start.3
  18.6 4.9 copy-start.4
  18.7 4.9 copy-start.2
  23.7 4.2 collective-permute-start.3
  27.0 4.2 collective-permute-start.2
  34.6 2.5 collective-permute-start.5
  35.0 4.2 collective-permute-start.4
  57.1 7.5 %collective-permute-start.9 = (bf16[2,2,128,256]{3,2,0,1:T(8,128)(2,1)S(1)}, bf16[2,2,128,256]{3,2,0,1:T(8,128)(2,1)S(1)}, u32[]{:S(2)}, u32[]{:S(2)}) collective-permute-start(bf16[2,2,128,256]{3,2,0,1:T(8,128)(2,1)S(1)} %get-tuple-element.325), channel_id=1, source_target_pairs={{4,0},{8,4},{12,8},{0,12},{5,1},{9,5},{13,9},{1,13},{6,2},{10,6},{... | collective-permute-start | bytes 786440 | tf_op jit(solution)/shard_map/ppermute | solution.py:22
  58.0 8.5 %collective-permute-start.8 = (bf16[2,2,128,256]{3,2,0,1:T(8,128)(2,1)S(1)}, bf16[2,2,128,256]{3,2,0,1:T(8,128)(2,1)S(1)}, u32[]{:S(2)}, u32[]{:S(2)}) collective-permute-start(bf16[2,2,128,256]{3,2,0,1:T(8,128)(2,1)S(1)} %get-tuple-element.325), channel_id=1, source_target_pairs={{0,4},{4,8},{8,12},{12,0},{1,5},{5,9},{9,13},{13,1},{2,6},{6,10},{... | collective-permute-start | bytes 786440 | tf_op jit(solution)/shard_map/ppermute | solution.py:19
  79.4 5.5 collective-permute-start.11
  80.8 12.8 %collective-permute-start.10 = (bf16[2,2,128,256]{3,2,0,1:T(8,128)(2,1)S(1)}, bf16[2,2,128,256]{3,2,0,1:T(8,128)(2,1)S(1)}, u32[]{:S(2)}, u32[]{:S(2)}) collective-permute-start(bf16[2,2,128,256]{3,2,0,1:T(8,128)(2,1)S(1)} %get-tuple-element.322), channel_id=1, source_target_pairs={{0,4},{4,8},{8,12},{12,0},{1,5},{5,9},{9,13},{13,1},{2,6},{6,10},{... | collective-permute-start | bytes 786440 | tf_op jit(solution)/shard_map/ppermute | solution.py:19
  256.8 1.9 copy-start
  571.8 7.2 %copy-start.1 = (f32[8,128,128]{1,2,0:T(8,128)S(1)}, f32[8,128,128]{1,2,0:T(8,128)}, u32[]{:S(2)}) copy-start(f32[8,128,128]{1,2,0:T(8,128)} %custom-call.70) | copy-start | bytes 1572868
  595.5 24.2 %all-to-all-start.1 = ((f32[4,1,65536]{2,1,0:T(1,128)}), f32[4,1,65536]{2,1,0:T(1,128)S(1)}, u32[]{:S(2)}, u32[]{:S(2)}) async-start(f32[4,1,65536]{2,1,0:T(1,128)} %reshape.847), calls=%async_computation.1 | async-start | bytes 2097152 | tf_op jit(solution)/shard_map/all_to_all | solution.py:160
Sparse Core Ops, SparseCore 0:
  133.6 107.9 all-reduce.2
where the time goes:
time: 647 us; the launch traced here: 640 us
  other arithmetic  287 us (44%)
  waiting for transfers between devices  130 us (20%)
  matrix products  87.6 us (14%)
  local copies, waits for them, and re-layouts  71.5 us (11%)
  starting transfers between devices  21.9 us (3%)
  blocking collectives  21.8 us (3%)
  between operations  20.3 us (3%)
    another operation x31, other arithmetic, body(): factor = jnp.linalg.cholesky(gram * gram_scale)  173 us
    psum x1, waiting for transfers between devices, body(): gram = lax.psum(partial_value, ('space', 'tangent'))  108 us
    another operation x3, other arithmetic, body(): jax.scipy.linalg.solve_triangular(factor, flat_rows.T, lower=True)  86 us
    another operation x14, matrix products, body(): factor = jnp.linalg.cholesky(gram * gram_scale)  23.1 us
    another operation x24, local copies, waits for them, and re-layouts  23 us
    all_to_all x1, blocking collectives, body(): lax.all_to_all(final, 'tangent', split_axis=2, concat_axis=3, tiled=True)  21.8 us
    gather x1, local copies, waits for them, and re-layouts, body(): log_diag = jnp.log(jnp.diagonal(factor))  17.3 us
    another operation x15, matrix products, body(): jax.scipy.linalg.solve_triangular(factor, flat_rows.T, lower=True)  14.7 us
  transfers between devices with their start and end apart: 14, of which 9 were waited for; matrix products, arithmetic and copies ran while one was open for 6% of the time, Pallas kernels for 0%

commit v1 on v0

--- a/solution.py
+++ b/solution.py
@@ -154,7 +154,7 @@
         preferred_element_type=jnp.float32,
     )
     gram_scale = 1.0 / (4.0 * slot_count * cell_total * lax.axis_size("space"))
-    gram = lax.psum(partial_value, ("space", "tangent"))
+    gram = lax.psum(lax.psum(partial_value, "tangent"), "space")
     factor = jnp.linalg.cholesky(gram * gram_scale)
     solved = jax.scipy.linalg.solve_triangular(factor, flat_rows.T, lower=True).T
     columns_out = lax.all_to_all(

time: 647 us -> 775 us (1.20)
  waiting for transfers between devices: 130 us -> 263 us
    psum x1 -> x2, waiting for transfers between devices: 108 us -> 240 us  [body(): gram = lax.psum(lax.psum(partial_value, 'tangent'), 'space')]
  transfers between devices with their start and end apart: 14 -> 15, of which waited for: 9 -> 10; matrix products, arithmetic and copies ran while one was open for 6% -> 5% of each run, Pallas kernels for 0% -> 0%
where the time goes in v1:
time: 775 us; the launch traced here: 768 us
  other arithmetic  286 us (37%)
  waiting for transfers between devices  263 us (34%)
  matrix products  84.9 us (11%)
  local copies, waits for them, and re-layouts  71.5 us (9%)
  blocking collectives  21.8 us (3%)
  starting transfers between devices  20.8 us (3%)
  between operations  20.3 us (3%)
    psum x2, waiting for transfers between devices, body(): gram = lax.psum(lax.psum(partial_value, 'tangent'), 'space')  240 us
    another operation x31, other arithmetic, body(): factor = jnp.linalg.cholesky(gram * gram_scale)  173 us
    another operation x3, other arithmetic, body(): jax.scipy.linalg.solve_triangular(factor, flat_rows.T, lower=True)  85.4 us
    another operation x14, matrix products, body(): factor = jnp.linalg.cholesky(gram * gram_scale)  23.1 us
    another operation x24, local copies, waits for them, and re-layouts  23 us
    all_to_all x1, blocking collectives, body(): lax.all_to_all(final, 'tangent', split_axis=2, concat_axis=3, tiled=True)  21.8 us
    gather x1, local copies, waits for them, and re-layouts, body(): log_diag = jnp.log(jnp.diagonal(factor))  17.3 us
  transfers between devices with their start and end apart: 15, of which 10 were waited for; matrix products, arithmetic and copies ran while one was open for 5% of the time, Pallas kernels for 0%

profile of v1, /device:TPU:1, one launch (start us, length us, event | category | flops | bytes accessed | tf_op | source)
XLA Modules:
  0.0 768.2 jit_solution(7363150155849417776)
XLA Ops:
  8.1 4.2 collective-permute-start.1
  14.4 3.3 collective-permute-start.7
  20.4 3.1 convert_reduce_fusion.79
  23.7 3.3 collective-permute-start.3
  27.9 3.4 collective-permute-done.2
  31.3 3.1 convert_reduce_fusion.52
  37.1 2.1 collective-permute-done.4
  39.3 3.3 convert_reduce_fusion.25
  59.8 4.8 collective-permute-done.9
  82.1 2.7 collective-permute-done.11
  86.5 7.0 collective-permute-done.10
  105.5 21.8 %all_to_all.33 = f32[2,4,128,256]{3,0,1,2:T(2,128)S(1)} all-to-all(f32[2,4,128,256]{3,0,1,2:T(2,128)S(1)} %copy.18), channel_id=1, replica_groups=mesh['groups'=2,'space'=4,'tangent'=4] {'tangent'}, dimensions={2} | all-to-all | bytes 2097152 | tf_op jit(solution)/shard_map/all_to_all | solution.py:146
  128.2 5.1 fusion.2420
  133.4 83.1 %all-reduce.4.cloned.1.call-done = f32[1024,1024]{0,1:T(8,128)} async-done(((f32[1024,1024]{0,1:T(8,128)}), f32[1024,1024]{0,1:T(8,128)}) %all-reduce.4.cloned.1.call-update) | async-done | bytes 4194320 | tf_op jit(solution)/shard_map/psum | solution.py:157
  216.9 157.4 %all-reduce.6.cloned.1.call-done = f32[1024,1024]{0,1:T(8,128)} async-done(((f32[1024,1024]{0,1:T(8,128)}), f32[1024,1024]{0,1:T(8,128)}) %all-reduce.6.cloned.1.call-update) | async-done | bytes 4194320 | tf_op jit(solution)/shard_map/psum | solution.py:157
  374.3 5.0 broadcast_multiply_fusion
  379.3 5.7 copy.21
  385.1 4.4 fusion
  389.5 1.9 copy-done
  391.5 11.7 %cholesky.187 = f32[128,128]{1,0:T(8,128)S(1)} custom-call(f32[128,128]{1,0:T(8,128)S(1)} %cholesky.514), custom_call_target="Cholesky" | custom-call | tf_op jit(solution)/shard_map/jit(cholesky)/cholesky | solution.py:158
  403.8 9.8 %custom-call.63 = f32[1,128,128]{1,2,0:T(8,128)S(1)} custom-call(f32[1,128,128]{2,1,0:T(8,128)S(1)} %get-tuple-element.432), custom_call_target="InvertDiagBlocksLowerTriangular" | custom-call | tf_op jit(solution)/shard_map/jit(cholesky)/cholesky | solution.py:158
  413.7 2.5 cholesky.218
  416.2 2.3 constant_dynamic-update-slice_fusion.32
  418.5 1.5 convolution_subtract_fusion
  420.1 11.9 %cholesky.209 = f32[128,128]{1,0:T(8,128)S(1)} custom-call(f32[128,128]{1,0:T(8,128)S(1)} %cholesky.518), custom_call_target="Cholesky" | custom-call | tf_op jit(solution)/shard_map/jit(cholesky)/cholesky | solution.py:158
  433.2 9.8 %custom-call.64 = f32[1,128,128]{1,2,0:T(8,128)S(1)} custom-call(f32[1,128,128]{2,1,0:T(8,128)S(1)} %get-tuple-element.429), custom_call_target="InvertDiagBlocksLowerTriangular" | custom-call | tf_op jit(solution)/shard_map/jit(cholesky)/cholesky | solution.py:158
  444.3 2.1 convolution_subtract_fusion.1
  446.4 11.7 %cholesky.402 = f32[128,128]{1,0:T(8,128)S(1)} custom-call(f32[128,128]{1,0:T(8,128)S(1)} %cholesky.523), custom_call_target="Cholesky" | custom-call | tf_op jit(solution)/shard_map/jit(cholesky)/cholesky | solution.py:158
  459.4 9.8 %custom-call.65 = f32[1,128,128]{1,2,0:T(8,128)S(1)} custom-call(f32[1,128,128]{2,1,0:T(8,128)S(1)} %get-tuple-element.426), custom_call_target="InvertDiagBlocksLowerTriangular" | custom-call | tf_op jit(solution)/shard_map/jit(cholesky)/cholesky | solution.py:158
  470.4 2.4 convolution_subtract_fusion.2
  472.8 11.9 %cholesky.421 = f32[128,128]{1,0:T(8,128)S(1)} custom-call(f32[128,128]{1,0:T(8,128)S(1)} %cholesky.528), custom_call_target="Cholesky" | custom-call | tf_op jit(solution)/shard_map/jit(cholesky)/cholesky | solution.py:158
  486.0 9.8 %custom-call.66 = f32[1,128,128]{1,2,0:T(8,128)S(1)} custom-call(f32[1,128,128]{2,1,0:T(8,128)S(1)} %get-tuple-element.423), custom_call_target="InvertDiagBlocksLowerTriangular" | custom-call | tf_op jit(solution)/shard_map/jit(cholesky)/cholesky | solution.py:158
  496.9 2.3 convolution_subtract_fusion.3
  499.3 11.7 %cholesky.440 = f32[128,128]{1,0:T(8,128)S(1)} custom-call(f32[128,128]{1,0:T(8,128)S(1)} %cholesky.533), custom_call_target="Cholesky" | custom-call | tf_op jit(solution)/shard_map/jit(cholesky)/cholesky | solution.py:158
  512.4 10.2 %custom-call.67 = f32[1,128,128]{1,2,0:T(8,128)S(1)} custom-call(f32[1,128,128]{2,1,0:T(8,128)S(1)} %get-tuple-element.420), custom_call_target="InvertDiagBlocksLowerTriangular" | custom-call | tf_op jit(solution)/shard_map/jit(cholesky)/cholesky | solution.py:158
  523.6 2.3 convolution_subtract_fusion.4
  525.9 11.7 %cholesky.460 = f32[128,128]{1,0:T(8,128)S(1)} custom-call(f32[128,128]{1,0:T(8,128)S(1)} %cholesky.538), custom_call_target="Cholesky" | custom-call | tf_op jit(solution)/shard_map/jit(cholesky)/cholesky | solution.py:158
  538.9 9.8 %custom-call.68 = f32[1,128,128]{1,2,0:T(8,128)S(1)} custom-call(f32[1,128,128]{2,1,0:T(8,128)S(1)} %get-tuple-element.417), custom_call_target="InvertDiagBlocksLowerTriangular" | custom-call | tf_op jit(solution)/shard_map/jit(cholesky)/cholesky | solution.py:158
  549.6 2.0 convolution_subtract_fusion.11
  551.7 11.9 %cholesky.480 = f32[128,128]{1,0:T(8,128)S(1)} custom-call(f32[128,128]{1,0:T(8,128)S(1)} %cholesky.543), custom_call_target="Cholesky" | custom-call | tf_op jit(solution)/shard_map/jit(cholesky)/cholesky | solution.py:158
  564.8 9.8 %custom-call.69 = f32[1,128,128]{1,2,0:T(8,128)S(1)} custom-call(f32[1,128,128]{2,1,0:T(8,128)S(1)} %get-tuple-element.414), custom_call_target="InvertDiagBlocksLowerTriangular" | custom-call | tf_op jit(solution)/shard_map/jit(cholesky)/cholesky | solution.py:158
  575.5 1.8 convolution_subtract_fusion.13
  577.3 11.7 %cholesky.498 = f32[128,128]{1,0:T(8,128)S(1)} custom-call(f32[128,128]{1,0:T(8,128)S(1)} %convolution_subtract_fusion.13), custom_call_target="Cholesky" | custom-call | tf_op jit(solution)/shard_map/jit(cholesky)/cholesky | solution.py:158
  595.3 6.6 fusion.1
  601.9 23.2 %while.1 = (s32[]{:T(128)}, f32[1024,1024]{1,0:T(8,128)}, s32[8,2]{0,1:T(2,128)S(1)}, f32[8,128,128]{2,1,0:T(8,128)S(1)}, s32[]{:T(128)}) while((s32[]{:T(128)}, f32[1024,1024]{1,0:T(8,128)}, s32[8,2]{0,1:T(2,128)S(1)}, f32[8,128,128]{2,1,0:T(8,128)S(1)}, s32[]{:T(128)}) %tuple.396), condition=%wide.while_cond, body=%wide.while_body.sunk | while | flops 2 | bytes 131189 | solution.py:159
  602.5 2.3 bitcast_dynamic-update-slice_fusion.2
  605.5 2.3 bitcast_dynamic-update-slice_fusion.2
  608.4 2.3 bitcast_dynamic-update-slice_fusion.2
  611.3 2.3 bitcast_dynamic-update-slice_fusion.2
  614.2 2.3 bitcast_dynamic-update-slice_fusion.2
  617.1 2.3 bitcast_dynamic-update-slice_fusion.2
  620.0 2.3 bitcast_dynamic-update-slice_fusion.2
  622.9 2.2 bitcast_dynamic-update-slice_fusion.2
  625.1 78.8 %custom-call.70 = f32[8,128,128]{1,2,0:T(8,128)S(1)} custom-call(f32[8,128,128]{2,1,0:T(8,128)S(1)} %get-tuple-element.10), custom_call_target="InvertDiagBlocksLowerTriangular" | custom-call | tf_op jit(solution)/shard_map/jit(_solve_triangular)/triangular_solve | solution.py:159
  710.6 1.5 convolution_subtract_fusion.5
  712.4 1.5 convolution_subtract_fusion.9
  714.2 1.6 convolution_subtract_fusion.12
  716.5 3.1 copy.24
  719.6 5.3 reshape.847
  725.0 4.4 all-to-all-start.1
  730.1 17.3 %gather_fusion = f32[1024]{0:T(1024)S(1)} fusion(f32[1024,1024]{1,0:T(8,128)} %get-tuple-element.320, s32[1024]{0:T(1024)S(1)} %bitcast.397), kind=kCustom, calls=%fused_computation | custom fusion | bytes 16384 | tf_op jit(solution)/shard_map/jit(diagonal)/cond/branch_0_fun/gather | solution.py:163
  748.5 3.8 reduce.48
  752.3 4.2 reshape.848
  756.5 4.6 copy.25
  (287 shorter events, 89.3 us)
Async XLA Ops:
  7.2 209.4 %all-reduce.4.cloned.1.call-start = ((), (), s32[]{:S(2)}) async-start(), calls=%async_computation.2 | async-start | bytes 8388608 | tf_op jit(solution)/shard_map/psum | solution.py:157
  8.1 12.2 %collective-permute-start.1 = (f32[2,2,128]{2,1,0:T(2,128)S(1)}, f32[2,2,128]{2,1,0:T(2,128)S(1)}, u32[]{:S(2)}, u32[]{:S(2)}) collective-permute-start(f32[2,2,128]{2,1,0:T(2,128)S(1)} %pad_maximum_fusion.11), channel_id=1, source_target_pairs={{4,0},{8,4},{12,8},{0,12},{5,1},{9,5},{13,9},{1,13},{6,2},{10,6},{... | collective-permute-start | bytes 6152 | tf_op jit(solution)/shard_map/ppermute | solution.py:22
  12.3 8.1 %collective-permute-start = (f32[2,2,128]{2,1,0:T(2,128)S(1)}, f32[2,2,128]{2,1,0:T(2,128)S(1)}, u32[]{:S(2)}, u32[]{:S(2)}) collective-permute-start(f32[2,2,128]{2,1,0:T(2,128)S(1)} %pad_maximum_fusion.11), channel_id=1, source_target_pairs={{0,4},{4,8},{8,12},{12,0},{1,5},{5,9},{9,13},{13,1},{2,6},{6,10},{... | collective-permute-start | bytes 6152 | tf_op jit(solution)/shard_map/ppermute | solution.py:19
  14.4 28.2 %collective-permute-start.7 = (bf16[2,2,128,256]{3,2,0,1:T(8,128)(2,1)S(1)}, bf16[2,2,128,256]{3,2,0,1:T(8,128)(2,1)S(1)}, u32[]{:S(2)}, u32[]{:S(2)}) collective-permute-start(bf16[2,2,128,256]{3,2,0,1:T(8,128)(2,1)S(1)} %get-tuple-element.327), channel_id=1, source_target_pairs={{4,0},{8,4},{12,8},{0,12},{5,1},{9,5},{13,9},{1,13},{6,2},{10,6},{... | collective-permute-start | bytes 786440 | tf_op jit(solution)/shard_map/ppermute | solution.py:22
  17.7 26.6 %collective-permute-start.6 = (bf16[2,2,128,256]{3,2,0,1:T(8,128)(2,1)S(1)}, bf16[2,2,128,256]{3,2,0,1:T(8,128)(2,1)S(1)}, u32[]{:S(2)}, u32[]{:S(2)}) collective-permute-start(bf16[2,2,128,256]{3,2,0,1:T(8,128)(2,1)S(1)} %get-tuple-element.327), channel_id=1, source_target_pairs={{0,4},{4,8},{8,12},{12,0},{1,5},{5,9},{9,13},{13,1},{2,6},{6,10},{... | collective-permute-start | bytes 786440 | tf_op jit(solution)/shard_map/ppermute | solution.py:19
  18.6 4.9 copy-start.2
  18.6 4.9 copy-start.3
  18.7 4.9 copy-start.1
  23.7 4.2 collective-permute-start.3
  27.0 4.2 collective-permute-start.2
  34.6 2.5 collective-permute-start.5
  35.0 4.2 collective-permute-start.4
  57.1 7.5 collective-permute-start.9
  58.0 8.5 %collective-permute-start.8 = (bf16[2,2,128,256]{3,2,0,1:T(8,128)(2,1)S(1)}, bf16[2,2,128,256]{3,2,0,1:T(8,128)(2,1)S(1)}, u32[]{:S(2)}, u32[]{:S(2)}) collective-permute-start(bf16[2,2,128,256]{3,2,0,1:T(8,128)(2,1)S(1)} %get-tuple-element.325), channel_id=1, source_target_pairs={{0,4},{4,8},{8,12},{12,0},{1,5},{5,9},{9,13},{13,1},{2,6},{6,10},{... | collective-permute-start | bytes 786440 | tf_op jit(solution)/shard_map/ppermute | solution.py:19
  79.4 5.5 collective-permute-start.11
  80.8 12.8 %collective-permute-start.10 = (bf16[2,2,128,256]{3,2,0,1:T(8,128)(2,1)S(1)}, bf16[2,2,128,256]{3,2,0,1:T(8,128)(2,1)S(1)}, u32[]{:S(2)}, u32[]{:S(2)}) collective-permute-start(bf16[2,2,128,256]{3,2,0,1:T(8,128)(2,1)S(1)} %get-tuple-element.322), channel_id=1, source_target_pairs={{0,4},{4,8},{8,12},{12,0},{1,5},{5,9},{9,13},{13,1},{2,6},{6,10},{... | collective-permute-start | bytes 786440 | tf_op jit(solution)/shard_map/ppermute | solution.py:19
  133.4 240.9 %all-reduce.6.cloned.1.call-start = ((), (), s32[]{:S(2)}) async-start(), calls=%async_computation.3 | async-start | bytes 8388608 | tf_op jit(solution)/shard_map/psum | solution.py:157
  389.5 1.9 copy-start
  725.0 23.0 %all-to-all-start.1 = ((f32[4,1,65536]{2,1,0:T(1,128)}), f32[4,1,65536]{2,1,0:T(1,128)S(1)}, u32[]{:S(2)}, u32[]{:S(2)}) async-start(f32[4,1,65536]{2,1,0:T(1,128)} %reshape.847), calls=%async_computation.1 | async-start | bytes 2097152 | tf_op jit(solution)/shard_map/all_to_all | solution.py:160
Sparse Core Ops, SparseCore 0:
  133.5 82.9 all-reduce.3
  219.0 155.2 all-reduce.5
